TPU v7x, 512 devices: a whole 4x4x16 slice. The times are simulated.
512 devices in a mesh: space: 128 (over z, x, core), basis: 4 (over y).
Axes of the slice: x: 4, y: 4, z: 16, core: 2. Of those that a mesh axis runs over, the one named last changes fastest.
Arguments:
- x_block: float32 [16, 3, 128, 32, 128], P(None, None, 'space', 'basis'), may hold values from -68 to 68
- basis: float32 [64, 3, 128, 32, 128], P('basis', None, 'space'), may hold values from -11 to 11
- material: int32 [128, 32, 128], P('space', 'basis'), may hold values from 0 to 7
- k0_blocks: float32 [8, 7, 3, 3], replicated, may hold values from -4 to 4
- k0_diag: float32 [8, 3], replicated, may hold values from 2 to 8
- ke_blocks: float32 [8, 7, 3, 3], replicated, may hold values from -6 to 6
- mass: float32 [8, 3], replicated, may hold values from 0.5 to 2
- velocities: float32 [1024], replicated, may hold values from 0.5 to 1
- shifts: float32 [1024], replicated, may hold values from 0.5 to 1.5
- sample: int32 [1], replicated, may hold values from 0 to 1023
Outputs:
- orthonormal: float32 [16, 3, 128, 32, 128], P(None, None, 'space', 'basis')
- coefficients: float32 [64, 16], P('basis')
- upper_factor: float32 [16, 16], replicated
All inputs are finite; a program needn't handle non-finite values.
Results may differ from a plain program's by a relative error of at most 0.00015.
Values sent between devices are 32-bit elements; how exact they have to be, the bound alone decides.
A program may use at most 64 MiB of HBM per device.

v0:
```python
import jax
import jax.numpy as jnp
from jax import lax
from jax.sharding import PartitionSpec as P

exact_precision = lax.Precision.HIGHEST


def with_halo(cells, sides, width):
    for axis, dim in sides:
        count = lax.axis_size(axis)
        ends = count - 1
        head = lax.slice_in_dim(cells, 0, width, axis=dim)
        tail = lax.slice_in_dim(cells, cells.shape[dim] - width, cells.shape[dim], axis=dim)
        cells = jnp.concatenate(
            [
                lax.ppermute(tail, axis, [(i, (i + 1) % count) for i in range(ends)]),
                cells,
                lax.ppermute(head, axis, [((i + 1) % count, i) for i in range(ends)]),
            ],
            axis=dim,
        )
    return cells


def stencil_tables(k0_blocks, k0_diag, ke_blocks, mass, velocities, shifts, sample):
    velocity = jnp.take(velocities, sample, axis=0)[0]
    sigma_value = jnp.take(shifts, sample, axis=0)[0]
    center = (k0_diag - sigma_value * mass)[:, :, None] * jnp.eye(3, dtype=jnp.float32)
    tables = k0_blocks - velocity * velocity * ke_blocks
    return tables.at[:, 0].add(center)


def neighbour_views(rimmed):
    centre = rimmed[:, :, 1:-1, 1:-1, :]
    lower_x = rimmed[:, :, :-2, 1:-1, :]
    upper_x = rimmed[:, :, 2:, 1:-1, :]
    lower_y = rimmed[:, :, 1:-1, :-2, :]
    upper_y = rimmed[:, :, 1:-1, 2:, :]
    zero_col = jnp.zeros(centre.shape[:4] + (1,), centre.dtype)
    lower_z = jnp.concatenate((zero_col, centre[:, :, :, :, :-1]), axis=4)
    upper_z = jnp.concatenate((centre[:, :, :, :, 1:], zero_col), axis=4)
    return [centre, lower_x, upper_x, lower_y, upper_y, lower_z, upper_z]


def cell_fields(tables, material_cells):
    material_count = tables.shape[0]
    fields = jnp.zeros((7, 3, 3) + material_cells.shape, jnp.float32)
    for level in range(material_count):
        chosen = (material_cells == level).astype(jnp.float32)
        fields = fields + tables[level][:, :, :, None, None, None] * chosen[None, None, None]
    return fields


def apply_fields(rimmed, fields):
    stencil_views = neighbour_views(rimmed)
    sums = [None, None, None]
    for offset in range(7):
        view = stencil_views[offset]
        for row in range(3):
            term = fields[offset, row, 0][None] * view[:, 0]
            term = term + fields[offset, row, 1][None] * view[:, 1]
            term = term + fields[offset, row, 2][None] * view[:, 2]
            sums[row] = term if sums[row] is None else sums[row] + term
    return jnp.stack(sums, axis=1)


def fine_image(x_block, material, tables):
    rimmed = with_halo(x_block, (("space", 2), ("basis", 3)), 1)
    return apply_fields(rimmed, cell_fields(tables, material))


def group_sum(partial_value):
    return lax.psum(partial_value, "space")


def scaled_block(fine_block, gram_matrix):
    block_cols = fine_block.shape[0]
    lower_factor = jnp.linalg.cholesky(gram_matrix)
    inverse = jax.scipy.linalg.solve_triangular(
        lower_factor, jnp.eye(block_cols, dtype=jnp.float32), lower=True
    ).T
    orthonormal = jnp.einsum("mcxyz,mn->ncxyz", fine_block, inverse, precision=exact_precision)
    return (orthonormal, lower_factor.T)


def finish(fine_block, row_count):
    gram_partial = jnp.einsum("ncxyz,mcxyz->nm", fine_block, fine_block, precision=exact_precision)
    gram_matrix = lax.psum(gram_partial, ("space", "basis")) / row_count
    return scaled_block(fine_block, gram_matrix)


def shards(
    x_block, basis, material, k0_blocks, k0_diag, ke_blocks, mass, velocities, shifts, sample
):
    tables = stencil_tables(k0_blocks, k0_diag, ke_blocks, mass, velocities, shifts, sample)
    block_cols = x_block.shape[0]
    extent_x = x_block.shape[2]
    extent_z = x_block.shape[4]
    full_y = basis.shape[3]
    group_cols = basis.shape[0]
    row_count = 3.0 * extent_x * lax.axis_size("space") * full_y * extent_z
    running = jnp.zeros((group_cols, block_cols), jnp.float32)
    fine_block = fine_image(x_block, material, tables)
    for repeat in range(2):
        partial_value = jnp.einsum(
            "kcxyz,ncxyz->kn",
            basis,
            lax.all_gather(fine_block, "basis", axis=3, tiled=True),
            precision=exact_precision,
        )
        local_coeffs = group_sum(partial_value) / row_count
        correction = jnp.einsum("kcxyz,kn->ncxyz", basis, local_coeffs, precision=exact_precision)
        fine_block = fine_block - lax.psum_scatter(
            correction, "basis", scatter_dimension=3, tiled=True
        )
        running = running + local_coeffs
    orthonormal, upper_factor = finish(fine_block, row_count)
    return (orthonormal, running, upper_factor)


def solution(mesh):
    in_specs = (
        P(None, None, "space", "basis", None),
        P("basis", None, "space", None, None),
        P("space", "basis", None),
        P(),
        P(),
        P(),
        P(),
        P(),
        P(),
        P(),
    )
    out_specs = (P(None, None, "space", "basis", None), P("basis", None), P())
    return jax.shard_map(shards, mesh=mesh, in_specs=in_specs, out_specs=out_specs, check_vma=False)
```

profile of v0, /device:TPU:1, one launch (start us, length us, event | category | flops | bytes accessed | tf_op | source)
XLA Modules:
  0.0 749.9 jit_solution(10074327521690366731)
XLA Ops:
  7.3 1.0 copy.71
  8.3 8.8 %collective-permute-start.1 = (f32[16,3,1,8,128]{4,0,3,1,2:T(8,128)S(1)}, f32[16,3,1,8,128]{4,0,3,1,2:T(8,128)S(1)}, u32[]{:S(2)}, u32[]{:S(2)}) collective-permute-start(f32[16,3,1,8,128]{4,0,3,1,2:T(8,128)S(1)} %copy.71), channel_id=1, source_target_pairs={{4,0},{8,4},{12,8},{16,12},{20,16},{24,20},{28,24},{32,28},{36,32}... | collective-permute-start | bytes 589832 | tf_op jit(solution)/shard_map/ppermute | solution.py:19
  17.1 1.9 collective-permute-start
  19.7 1.3 dynamic-slice.13
  21.0 1.3 dynamic-slice.12
  24.7 0.6 multiply_add_fusion
  25.6 0.9 copy-done.1
  26.6 1.3 collective-permute-start.3
  27.9 4.0 collective-permute-start.2
  31.9 1.4 collective-permute-done.2
  33.9 11.9 %all_gather.6 = f32[16,3,1,32,128]{4,0,3,1,2:T(8,128)S(1)} all-gather(f32[16,3,1,8,128]{4,0,3,1,2:T(8,128)S(1)} %pad_maximum_fusion), channel_id=1, replica_groups=mesh['space'=128,'basis'=4] {'basis'}, dimensions={3}, use_global_device_ids=true | all-gather | bytes 983040 | tf_op jit(solution)/shard_map/all_gather | solution.py:109
  45.8 1.4 convolution_bitcast_fusion.4
  47.2 256.7 %psum.21 = f32[16,16]{0,1:T(8,128)S(1)} all-reduce(f32[16,16]{0,1:T(8,128)S(1)} %convolution_bitcast_fusion.4), channel_id=1, replica_groups=mesh['space'=128,'basis'=4] {'space'}, use_global_device_ids=true, to_apply=%region_0.1 | all-reduce | flops 256 | bytes 2048 | tf_op jit(solution)/shard_map/psum | solution.py:74
  303.9 1.1 convolution_bitcast_fusion.1
  305.1 1.1 copy.129
  306.3 26.9 %reduce-scatter.9.cloned.1.call-done = f32[8,6144]{1,0:T(8,128)} async-done(((f32[32,6144]{1,0:T(8,128)}), f32[8,6144]{1,0:T(8,128)}) %reduce-scatter.9.cloned.1.call-update) | async-done | bytes 196624
  333.2 1.0 copy.108
  334.2 11.1 %all_gather.7 = f32[16,3,1,32,128]{4,0,3,1,2:T(8,128)S(1)} all-gather(f32[16,3,1,8,128]{4,0,3,1,2:T(8,128)S(1)} %copy_subtract_fusion.1), channel_id=1, replica_groups=mesh['space'=128,'basis'=4] {'basis'}, dimensions={3}, use_global_device_ids=true | all-gather | bytes 983040 | tf_op jit(solution)/shard_map/all_gather | solution.py:109
  345.3 1.4 convolution_bitcast_fusion.3
  346.7 256.0 %psum.22 = f32[16,16]{0,1:T(8,128)S(1)} all-reduce(f32[16,16]{0,1:T(8,128)S(1)} %convolution_bitcast_fusion.3), channel_id=1, replica_groups=mesh['space'=128,'basis'=4] {'space'}, use_global_device_ids=true, to_apply=%region_2.3 | all-reduce | flops 256 | bytes 2048 | tf_op jit(solution)/shard_map/psum | solution.py:74
  602.7 1.1 convolution_bitcast_fusion
  603.9 1.1 copy.128
  605.1 0.7 copy.86
  605.8 24.7 %reduce-scatter.11.cloned.1.call-done = f32[8,6144]{1,0:T(8,128)} async-done(((f32[32,6144]{1,0:T(8,128)}), f32[8,6144]{1,0:T(8,128)}) %reduce-scatter.11.cloned.1.call-update) | async-done | bytes 196624
  630.5 1.0 copy.110
  631.8 105.2 %psum.23 = f32[16,16]{0,1:T(8,128)S(1)} all-reduce(f32[16,16]{0,1:T(8,128)S(1)} %convolution_bitcast_fusion.6), channel_id=1, replica_groups=mesh['space'=128,'basis'=4] {'space','basis'}, use_global_device_ids=true, to_apply=%region_4.5 | all-reduce | flops 256 | bytes 2048 | tf_op jit(solution)/shard_map/psum | solution.py:89
  737.1 1.5 cholesky.17
  738.6 0.6 compare_reduce_fusion
  739.2 0.6 fusion.15
  739.9 0.7 copy.87
  740.6 1.2 custom-call.7
  742.3 0.7 copy.85
  (59 shorter events, 3.2 us)
Async XLA Ops:
  7.2 38.7 %copy-start = (f32[16,3,1,32,128]{4,3,2,1,0:T(8,128)S(1)}, f32[16,3,1,32,128]{4,3,2,1,0:T(8,128)}, u32[]{:S(2)}) copy-start(f32[16,3,1,32,128]{4,3,2,1,0:T(8,128)} %param.13) | copy-start | bytes 2359300
  7.2 326.0 %reduce-scatter.9.cloned.1.call-start = ((), (), s32[]{:S(2)}) async-start(), calls=%async_computation.2 | async-start | bytes 983040
  7.2 16.3 %copy-start.4 = (s32[1,8,128]{2,1,0:T(8,128)S(1)}, s32[1,8,128]{2,1,0:T(8,128)}, u32[]{:S(2)}) copy-start(s32[1,8,128]{2,1,0:T(8,128)} %param.14) | copy-start | bytes 12292
  7.2 16.3 %copy-start.5 = (f32[8,3]{0,1:T(4,128)S(1)}, f32[8,3]{0,1:T(4,128)}, u32[]{:S(2)}) copy-start(f32[8,3]{0,1:T(4,128)} %param.16) | copy-start | bytes 292
  7.2 16.3 %copy-start.6 = (f32[8,3]{0,1:T(4,128)S(1)}, f32[8,3]{0,1:T(4,128)}, u32[]{:S(2)}) copy-start(f32[8,3]{0,1:T(4,128)} %param.18) | copy-start | bytes 292
  8.3 18.2 %collective-permute-start.1 = (f32[16,3,1,8,128]{4,0,3,1,2:T(8,128)S(1)}, f32[16,3,1,8,128]{4,0,3,1,2:T(8,128)S(1)}, u32[]{:S(2)}, u32[]{:S(2)}) collective-permute-start(f32[16,3,1,8,128]{4,0,3,1,2:T(8,128)S(1)} %copy.71), channel_id=1, source_target_pairs={{4,0},{8,4},{12,8},{16,12},{20,16},{24,20},{28,24},{32,28},{36,32}... | collective-permute-start | bytes 589832 | tf_op jit(solution)/shard_map/ppermute | solution.py:19
  17.1 8.5 %collective-permute-start = (f32[16,3,1,8,128]{4,0,3,1,2:T(8,128)S(1)}, f32[16,3,1,8,128]{4,0,3,1,2:T(8,128)S(1)}, u32[]{:S(2)}, u32[]{:S(2)}) collective-permute-start(f32[16,3,1,8,128]{4,0,3,1,2:T(8,128)S(1)} %copy.71), channel_id=1, source_target_pairs={{0,4},{4,8},{8,12},{12,16},{16,20},{20,24},{24,28},{28,32},{32,36}... | collective-permute-start | bytes 589832 | tf_op jit(solution)/shard_map/ppermute | solution.py:17
  19.0 4.6 copy-start.3
  19.0 4.6 copy-start.2
  25.5 0.9 copy-start.1
  26.6 5.3 collective-permute-start.3
  27.9 5.4 collective-permute-start.2
  306.3 324.3 %reduce-scatter.11.cloned.1.call-start = ((), (), s32[]{:S(2)}) async-start(), calls=%async_computation.3 | async-start | bytes 983040
Sparse Core Ops, SparseCore 0:
  306.4 26.7 reduce-scatter.8
  605.2 25.2 reduce-scatter.10
where the time goes:
time: 750 us
  blocking collectives  641 us (85%)
  waiting for transfers between devices  53 us (7%)
  between operations  16.4 us (2%)
  starting transfers between devices  16.1 us (2%)
  local copies, waits for them, and re-layouts  12.2 us (2%)
    psum x2, blocking collectives, group_sum(): return lax.psum(partial_value, 'space')  513 us
    psum x1, blocking collectives, finish(): gram_matrix = lax.psum(gram_partial, ('space', 'basis')) / row_count  105 us
    unnamed x4, waiting for transfers between devices  51.6 us
    all_gather x2, blocking collectives, shards(): lax.all_gather(fine_block, 'basis', axis=3, tiled=True)  23 us
  transfers between devices with their start and end apart: 6, of which 3 were waited for; matrix products, arithmetic and copies ran while one was open for 1% of the time, Pallas kernels for 0%

commit v1 on v0

--- a/solution.py
+++ b/solution.py
@@ -86,7 +86,7 @@
 
 def finish(fine_block, row_count):
     gram_partial = jnp.einsum("ncxyz,mcxyz->nm", fine_block, fine_block, precision=exact_precision)
-    gram_matrix = lax.psum(gram_partial, ("space", "basis")) / row_count
+    gram_matrix = lax.psum(lax.psum(gram_partial, "basis"), "space") / row_count
     return scaled_block(fine_block, gram_matrix)
 
 

time: 750 us -> 907 us (1.21)
  blocking collectives: 641 us -> 797 us
    psum x1 -> x2, blocking collectives: 105 us -> 262 us  [finish(): gram_matrix = lax.psum(lax.psum(gram_partial, 'basis'), 'space') / row_count]
where the time goes in v1:
time: 907 us; the launch traced here: 906 us
  blocking collectives  797 us (88%)
  waiting for transfers between devices  53 us (6%)
  between operations  16.4 us (2%)
  starting transfers between devices  16.1 us (2%)
  local copies, waits for them, and re-layouts  12.2 us (1%)
    psum x2, blocking collectives, group_sum(): return lax.psum(partial_value, 'space')  513 us
    psum x2, blocking collectives, finish(): gram_matrix = lax.psum(lax.psum(gram_partial, 'basis'), 'space') / row_count  262 us
    unnamed x4, waiting for transfers between devices  51.6 us
    all_gather x2, blocking collectives, shards(): lax.all_gather(fine_block, 'basis', axis=3, tiled=True)  23 us
  transfers between devices with their start and end apart: 6, of which 3 were waited for; matrix products, arithmetic and copies ran while one was open for 1% of the time, Pallas kernels for 0%

profile of v1, /device:TPU:1, one launch (start us, length us, event | category | flops | bytes accessed | tf_op | source)
XLA Modules:
  0.0 906.2 jit_solution(14329624636834201894)
XLA Ops:
  7.3 1.0 copy.71
  8.3 8.8 collective-permute-start.1
  17.1 1.9 collective-permute-start
  19.7 1.3 dynamic-slice.13
  21.0 1.3 dynamic-slice.12
  25.6 0.9 copy-done.1
  26.6 1.3 collective-permute-start.3
  27.9 4.0 collective-permute-start.2
  31.9 1.4 collective-permute-done.2
  33.9 11.9 %all_gather.6 = f32[16,3,1,32,128]{4,0,3,1,2:T(8,128)S(1)} all-gather(f32[16,3,1,8,128]{4,0,3,1,2:T(8,128)S(1)} %pad_maximum_fusion), channel_id=1, replica_groups=mesh['space'=128,'basis'=4] {'basis'}, dimensions={3}, use_global_device_ids=true | all-gather | bytes 983040 | tf_op jit(solution)/shard_map/all_gather | solution.py:109
  45.8 1.4 convolution_bitcast_fusion.4
  47.2 256.7 %psum.28 = f32[16,16]{0,1:T(8,128)S(1)} all-reduce(f32[16,16]{0,1:T(8,128)S(1)} %convolution_bitcast_fusion.4), channel_id=1, replica_groups=mesh['space'=128,'basis'=4] {'space'}, use_global_device_ids=true, to_apply=%region_0.1 | all-reduce | flops 256 | bytes 2048 | tf_op jit(solution)/shard_map/psum | solution.py:74
  303.9 1.1 convolution_bitcast_fusion.1
  305.1 1.1 copy.129
  306.3 26.9 %reduce-scatter.9.cloned.1.call-done = f32[8,6144]{1,0:T(8,128)} async-done(((f32[32,6144]{1,0:T(8,128)}), f32[8,6144]{1,0:T(8,128)}) %reduce-scatter.9.cloned.1.call-update) | async-done | bytes 196624
  333.2 1.0 copy.108
  334.2 11.1 %all_gather.7 = f32[16,3,1,32,128]{4,0,3,1,2:T(8,128)S(1)} all-gather(f32[16,3,1,8,128]{4,0,3,1,2:T(8,128)S(1)} %copy_subtract_fusion.1), channel_id=1, replica_groups=mesh['space'=128,'basis'=4] {'basis'}, dimensions={3}, use_global_device_ids=true | all-gather | bytes 983040 | tf_op jit(solution)/shard_map/all_gather | solution.py:109
  345.3 1.4 convolution_bitcast_fusion.3
  346.7 256.0 %psum.29 = f32[16,16]{0,1:T(8,128)S(1)} all-reduce(f32[16,16]{0,1:T(8,128)S(1)} %convolution_bitcast_fusion.3), channel_id=1, replica_groups=mesh['space'=128,'basis'=4] {'space'}, use_global_device_ids=true, to_apply=%region_2.3 | all-reduce | flops 256 | bytes 2048 | tf_op jit(solution)/shard_map/psum | solution.py:74
  602.7 1.1 convolution_bitcast_fusion
  603.9 1.1 copy.128
  605.1 0.7 copy.86
  605.8 24.7 %reduce-scatter.11.cloned.1.call-done = f32[8,6144]{1,0:T(8,128)} async-done(((f32[32,6144]{1,0:T(8,128)}), f32[8,6144]{1,0:T(8,128)}) %reduce-scatter.11.cloned.1.call-update) | async-done | bytes 196624
  630.5 1.0 copy.110
  631.8 6.1 psum.30
  638.0 255.4 %psum.31 = f32[16,16]{0,1:T(8,128)S(1)} all-reduce(f32[16,16]{0,1:T(8,128)S(1)} %psum.30), channel_id=1, replica_groups=mesh['space'=128,'basis'=4] {'space'}, use_global_device_ids=true, to_apply=%region_5.6 | all-reduce | flops 256 | bytes 2048 | tf_op jit(solution)/shard_map/psum | solution.py:89
  893.4 1.5 cholesky.17
  894.9 0.6 compare_reduce_fusion
  895.6 0.6 fusion.15
  896.2 0.7 copy.87
  896.9 1.2 custom-call.7
  898.6 0.7 copy.85
  (60 shorter events, 3.9 us)
Async XLA Ops:
  7.2 38.7 %copy-start = (f32[16,3,1,32,128]{4,3,2,1,0:T(8,128)S(1)}, f32[16,3,1,32,128]{4,3,2,1,0:T(8,128)}, u32[]{:S(2)}) copy-start(f32[16,3,1,32,128]{4,3,2,1,0:T(8,128)} %param.13) | copy-start | bytes 2359300
  7.2 326.0 %reduce-scatter.9.cloned.1.call-start = ((), (), s32[]{:S(2)}) async-start(), calls=%async_computation.2 | async-start | bytes 983040
  7.2 16.3 %copy-start.4 = (s32[1,8,128]{2,1,0:T(8,128)S(1)}, s32[1,8,128]{2,1,0:T(8,128)}, u32[]{:S(2)}) copy-start(s32[1,8,128]{2,1,0:T(8,128)} %param.14) | copy-start | bytes 12292
  7.2 16.3 %copy-start.5 = (f32[8,3]{0,1:T(4,128)S(1)}, f32[8,3]{0,1:T(4,128)}, u32[]{:S(2)}) copy-start(f32[8,3]{0,1:T(4,128)} %param.16) | copy-start | bytes 292
  7.2 16.3 %copy-start.6 = (f32[8,3]{0,1:T(4,128)S(1)}, f32[8,3]{0,1:T(4,128)}, u32[]{:S(2)}) copy-start(f32[8,3]{0,1:T(4,128)} %param.18) | copy-start | bytes 292
  8.3 18.2 %collective-permute-start.1 = (f32[16,3,1,8,128]{4,0,3,1,2:T(8,128)S(1)}, f32[16,3,1,8,128]{4,0,3,1,2:T(8,128)S(1)}, u32[]{:S(2)}, u32[]{:S(2)}) collective-permute-start(f32[16,3,1,8,128]{4,0,3,1,2:T(8,128)S(1)} %copy.71), channel_id=1, source_target_pairs={{4,0},{8,4},{12,8},{16,12},{20,16},{24,20},{28,24},{32,28},{36,32}... | collective-permute-start | bytes 589832 | tf_op jit(solution)/shard_map/ppermute | solution.py:19
  17.1 8.5 collective-permute-start
  19.0 4.6 copy-start.3
  19.0 4.6 copy-start.2
  25.5 0.9 copy-start.1
  26.6 5.3 collective-permute-start.3
  27.9 5.4 collective-permute-start.2
  306.3 324.3 %reduce-scatter.11.cloned.1.call-start = ((), (), s32[]{:S(2)}) async-start(), calls=%async_computation.3 | async-start | bytes 983040
Sparse Core Ops, SparseCore 0:
  306.4 26.7 reduce-scatter.8
  605.2 25.2 reduce-scatter.10
